TPU v7x, 256 devices: a whole 4x4x8 slice. The times are simulated.
256 devices in a mesh: rows: 32 (over x, y, core), cols: 8 (over z).
Axes of the slice: x: 4, y: 4, z: 8, core: 2. Of those that a mesh axis runs over, the one named last changes fastest.
Arguments:
- fblocks: bfloat16 [512, 20, 128, 128], P('rows'), may hold values from -0.15625 to 0.15625
- fcol: int32 [512, 20], P('rows'), may hold values from 0 to 511, as said below
- zblocks: bfloat16 [512, 8, 128, 128], P('rows', 'cols'), may hold values from -0.5 to 0.5
- zcol: int32 [512, 8], P('rows', 'cols'), may hold values from 0 to 1, as said below
Outputs:
- f_orth: float32 [2048, 2048], P('rows', 'cols')
Inputs may be any that keep to these rules, and one draw needn't show every extreme that they name: `fcol`: each block row r lists 20 distinct block rows; the first is r itself, every other g satisfies (g - r) mod 512 <= 48 or (r - g) mod 512 <= 48. `zcol`: within a block row, the 1 entries of one group are distinct.
All inputs are finite; a program needn't handle non-finite values.
Results may differ from a plain program's by a relative error of at most 0.0029.
Values may be sent and summed in bfloat16 or wider, within the bound.
A program may use at most 128 MiB of HBM per device.

v0:
```python
import jax
import jax.numpy as jnp
from jax import lax
from jax.sharding import PartitionSpec as P

K = 20
S = 1
REACH = 3
CB = 2


def from_behind(value, axis, steps):
    count = lax.axis_size(axis)
    pairs = [(source, (source + steps) % count) for source in range(count)]
    return lax.ppermute(value, axis, pairs)


def expand_slots(slot_blocks, slot_cols, width):
    count_rows = slot_blocks.shape[0]
    groups = slot_cols.shape[1] // S
    order = slot_blocks.shape[-1]
    slot_blocks = slot_blocks.reshape(count_rows, groups, S, order, order)
    slot_cols = slot_cols.reshape(count_rows, groups, S)
    target = jnp.arange(width, dtype=jnp.int32)
    match = slot_cols[:, :, 0, None] == target[None, None, :]
    chosen = jnp.where(
        match[:, :, :, None, None], slot_blocks[:, :, 0, None], jnp.zeros((), jnp.bfloat16)
    )
    return chosen.reshape(count_rows, groups * width, order, order)


def body(fblocks, fcol, zblocks, zcol):
    local_rows = fblocks.shape[0]
    order = fblocks.shape[-1]
    row_devices = lax.axis_size("rows")
    block_list = []
    column_list = []
    for offset in range(REACH, -REACH - 1, -1):
        if offset == 0:
            pieces = (zblocks, zcol)
        else:
            pieces = from_behind((zblocks, zcol), "rows", offset)
        block_list.append(pieces[0])
        column_list.append(pieces[1])
    fetched = jnp.concatenate(block_list, axis=0)
    fetched_cols = jnp.concatenate(column_list, axis=0)
    first_row = (lax.axis_index("rows") - REACH) * local_rows
    position = jnp.mod(fcol - first_row, local_rows * row_devices)
    chosen = jnp.take(fetched, position.reshape(-1), axis=0)
    chosen_cols = jnp.take(fetched_cols, position.reshape(-1), axis=0)
    expanded = expand_slots(chosen, chosen_cols, CB).reshape(local_rows, K, CB, order, order)
    product = jnp.einsum(
        "rkab,rkcbe->rcae", fblocks, expanded, preferred_element_type=jnp.float32
    ).astype(jnp.bfloat16)
    all_slots, all_cols = (
        lax.all_gather(zblocks, "cols", axis=1, tiled=True),
        lax.all_gather(zcol, "cols", axis=1, tiled=True),
    )
    dense_rows = expand_slots(all_slots, all_cols, CB)
    flat_rows = jnp.transpose(dense_rows, (0, 2, 1, 3)).reshape(local_rows, order, -1)
    summed = jnp.einsum("rak,rcae->kce", flat_rows, product, preferred_element_type=jnp.float32)
    return lax.psum_scatter(
        summed.reshape(flat_rows.shape[2] // row_devices * lax.axis_size("rows"), -1),
        "rows",
        scatter_dimension=0,
        tiled=True,
    )


def solution(mesh):
    in_specs = (
        P("rows", None, None, None),
        P("rows", None),
        P("rows", "cols", None, None),
        P("rows", "cols"),
    )
    out_specs = P("rows", "cols")
    return jax.shard_map(body, mesh=mesh, in_specs=in_specs, out_specs=out_specs, check_vma=False)
```

profile of v0, /device:TPU:5, one launch (start us, length us, event | category | flops | bytes accessed | tf_op | source)
XLA Modules:
  0.0 245.5 jit_solution(14592450667510525770)
XLA Ops:
  6.5 0.0 copy-start
  6.5 0.0 all-gather.3.cloned.1.call-start
  6.5 0.7 all-gather.3.cloned.1.call-update
  7.3 0.0 reduce-scatter.2.cloned.1.call-start
  7.3 3.6 %collective-permute-start = (s32[16,1]{0,1:T(1,128)}, s32[16,1]{0,1:T(1,128)S(1)}, u32[]{:S(2)}, u32[]{:S(2)}) collective-permute-start(s32[16,1]{0,1:T(1,128)} %param.7), channel_id=1, source_target_pairs={{0,24},{8,32},{16,40},{24,48},{32,56},{40,64},{48,72},{56,80},{64,... | collective-permute-start | bytes 200 | tf_op jit(solution)/shard_map/ppermute | solution.py:15
  10.9 0.4 collective-permute-start.1
  11.3 0.3 collective-permute-start.2
  11.6 0.2 collective-permute-start.3
  11.8 2.4 collective-permute-start.6
  14.2 0.7 add_select_fusion
  14.9 0.1 reshape.122
  15.0 0.1 eq.47
  15.1 16.5 %all-gather = s32[8,1,16]{2,1,0:T(1,128)S(1)} all-gather(s32[1,1,16]{2,1,0:T(1,128)} %bitcast.35), channel_id=1, replica_groups=mesh['rows'=32,'cols'=8] {'cols'}, dimensions={0}, use_global_device_ids=true | all-gather | bytes 576 | tf_op jit(solution)/shard_map/all_gather | solution.py:57
  31.6 0.1 broadcast_compare_fusion
  31.7 0.1 copy.11
  31.8 0.0 collective-permute-done
  31.8 2.5 %collective-permute-start.4 = (s32[16,1]{0,1:T(1,128)}, s32[16,1]{0,1:T(1,128)S(1)}, u32[]{:S(2)}, u32[]{:S(2)}) collective-permute-start(s32[16,1]{0,1:T(1,128)} %param.7), channel_id=1, source_target_pairs={{0,240},{8,248},{16,0},{24,8},{32,16},{40,24},{48,32},{56,40},{64,... | collective-permute-start | bytes 200 | tf_op jit(solution)/shard_map/ppermute | solution.py:15
  34.3 0.0 collective-permute-done.1
  34.3 3.0 %collective-permute-start.5 = (s32[16,1]{0,1:T(1,128)}, s32[16,1]{0,1:T(1,128)S(1)}, u32[]{:S(2)}, u32[]{:S(2)}) collective-permute-start(s32[16,1]{0,1:T(1,128)} %param.7), channel_id=1, source_target_pairs={{0,232},{8,240},{16,248},{24,0},{32,8},{40,16},{48,24},{56,32},{64... | collective-permute-start | bytes 200 | tf_op jit(solution)/shard_map/ppermute | solution.py:15
  37.3 0.0 collective-permute-done.2
  37.3 0.4 collective-permute-start.7
  37.7 0.0 collective-permute-done.3
  37.7 0.0 collective-permute-start.8
  37.8 0.0 collective-permute-done.4
  37.8 1.1 collective-permute-start.9
  38.9 0.1 collective-permute-done.5
  38.9 3.4 %collective-permute-start.10 = (bf16[16,1,128,128]{3,2,1,0:T(8,128)(2,1)}, bf16[16,1,128,128]{3,2,1,0:T(8,128)(2,1)S(1)}, u32[]{:S(2)}, u32[]{:S(2)}) collective-permute-start(bf16[16,1,128,128]{3,2,1,0:T(8,128)(2,1)} %param.6), channel_id=1, source_target_pairs={{0,240},{8,248},{16,0},{24,8},{32,16},{40,24},{48,32},{56,40},{64,... | collective-permute-start | bytes 1572872 | tf_op jit(solution)/shard_map/ppermute | solution.py:15
  42.3 0.7 concatenate.6
  43.1 2.4 gather_fusion
  45.4 0.1 gather.13
  45.5 0.7 broadcast_select_fusion.2
  46.3 0.0 collective-permute-done.6
  46.3 0.5 collective-permute-start.11
  46.8 0.8 constant_dynamic-update-slice_fusion.6
  47.6 6.6 %collective-permute-done.7 = bf16[16,1,128,128]{3,2,1,0:T(8,128)(2,1)S(1)} collective-permute-done((bf16[16,1,128,128]{3,2,1,0:T(8,128)(2,1)}, bf16[16,1,128,128]{3,2,1,0:T(8,128)(2,1)S(1)}, u32[]{:S(2)}, u32[]{:S(2)}) %collective-permute-start.7) | collective-permute-done | bytes 524320 | tf_op jit(solution)/shard_map/ppermute | solution.py:15
  54.2 0.8 constant_dynamic-update-slice_fusion.5
  55.0 0.4 collective-permute-done.8
  55.4 0.8 constant_dynamic-update-slice_fusion.4
  56.3 0.0 copy-done
  56.3 0.8 constant_dynamic-update-slice_fusion.3
  57.1 0.0 collective-permute-done.9
  57.1 0.9 constant_dynamic-update-slice_fusion.2
  57.9 2.1 collective-permute-done.10
  60.0 0.8 constant_dynamic-update-slice_fusion.1
  60.9 10.3 %collective-permute-done.11 = bf16[16,1,128,128]{3,2,1,0:T(8,128)(2,1)S(1)} collective-permute-done((bf16[16,1,128,128]{3,2,1,0:T(8,128)(2,1)}, bf16[16,1,128,128]{3,2,1,0:T(8,128)(2,1)S(1)}, u32[]{:S(2)}, u32[]{:S(2)}) %collective-permute-start.11) | collective-permute-done | bytes 524320 | tf_op jit(solution)/shard_map/ppermute | solution.py:15
  71.2 0.8 constant_dynamic-update-slice_fusion
  72.0 12.7 %gather_fusion.1 = bf16[320,128,128]{2,1,0:T(8,128)(2,1)} fusion(bf16[112,128,128]{2,1,0:T(8,128)(2,1)} %bitcast.8, s32[1024]{0:T(1024)S(1)} %pad_clamp_fusion), kind=kCustom, calls=%fused_computation.1 | custom fusion | bytes 20972800 | tf_op jit(solution)/shard_map/jit(_take)/gather | solution.py:49
  84.8 10.2 %broadcast_select_fusion = bf16[16,20,128,128]{3,2,1,0:T(8,128)(2,1)} fusion(bf16[16,20,128,128]{3,2,1,0:T(8,128)(2,1)} %bitcast.30, pred[16,20]{1,0:T(8,128)(4,1)S(1)} %get-tuple-element.6), kind=kLoop, calls=%fused_computation.8 | loop fusion | flops 5242880 | bytes 20971840 | tf_op jit(solution)/shard_map/jit(_take)/select_n | solution.py:49
  95.0 13.8 %copy.13 = bf16[16,20,128,128]{2,3,1,0:T(8,128)(2,1)} copy(bf16[16,20,128,128]{3,2,1,0:T(8,128)(2,1)} %broadcast_select_fusion) | data formatting | bytes 20971520 | tf_op jit(solution)/shard_map/jit(_take)/select_n | solution.py:49
  108.8 10.0 %bitcast_convert_fusion = bf16[16,2,128,128]{3,2,1,0:T(8,128)(2,1)S(1)} fusion(bf16[16,20,128,128]{3,2,1,0:T(8,128)(2,1)} %param.4, pred[16,20,2]{1,2,0:T(4,128)(4,1)S(1)} %iota_compare_fusion, bf16[16,20,128,128]{2,3,1,0:T(8,128)(2,1)} %copy.13), kind=kOutput, calls=%fused_computation.11 | convolution fusion | flops 2695364608 | bytes 22020736 | tf_op jit(solution)/shard_map/rkab,rkcbe->rcae/dot_general | solution.py:52
  118.7 0.0 all-gather.3.cloned.1.call-done
  118.8 6.3 %copy.12 = bf16[16,8,128,128]{2,3,1,0:T(8,128)(2,1)} copy(bf16[16,8,128,128]{3,2,1,0:T(8,128)(2,1)} %all-gather.3.cloned.1.call-done) | data formatting | bytes 8388608 | tf_op jit(solution)/shard_map/all_gather | solution.py:56
  125.1 8.6 %broadcast_in_dim.65 = bf16[16,8,2,128,128]{3,4,2,1,0:T(8,128)(2,1)} broadcast(bf16[16,8,128,128]{2,3,1,0:T(8,128)(2,1)} %copy.12), dimensions={0,1,3,4} | broadcast | bytes 12582912 | tf_op jit(solution)/shard_map/jit(_where)/broadcast_in_dim | solution.py:26
  133.6 7.3 %broadcast_select_fusion.1 = bf16[16,16,128,128]{2,3,1,0:T(8,128)(2,1)} fusion(bf16[16,16,128,128]{2,3,1,0:T(8,128)(2,1)} %bitcast.31, pred[16,16]{1,0:T(8,128)(4,1)S(1)} %copy.11), kind=kLoop, calls=%fused_computation.9 | loop fusion | flops 4194304 | bytes 16777472 | tf_op jit(solution)/shard_map/jit(_where)/select_n | solution.py:26
  140.9 7.1 %convolution_bitcast_fusion = f32[2048,256]{1,0:T(8,128)} fusion(bf16[16,128,2048]{1,2,0:T(8,128)(2,1)} %bitcast.32, bf16[256,128,16]{1,0,2:T(8,128)(2,1)S(1)} %bitcast.36), kind=kOutput, calls=%fused_computation.10 | convolution fusion | flops 2147483648 | bytes 11534336 | tf_op jit(solution)/shard_map/rak,rcae->kce/dot_general | solution.py:61
  148.0 0.0 reduce-scatter.2.cloned.1.call-update
  148.0 90.6 %reduce-scatter.2.cloned.1.call-done = f32[64,256]{1,0:T(8,128)} async-done(((f32[2048,256]{1,0:T(8,128)}), f32[64,256]{1,0:T(8,128)}) %reduce-scatter.2.cloned.1.call-update) | async-done | bytes 65552 | tf_op jit(solution)/shard_map/reduce_scatter | solution.py:62
  (5 shorter events, 0.0 us)
Async XLA Ops:
  6.5 49.7 %copy-start = (bf16[16,1,128,128]{3,2,1,0:T(8,128)(2,1)S(1)}, bf16[16,1,128,128]{3,2,1,0:T(8,128)(2,1)}, u32[]{:S(2)}) copy-start(bf16[16,1,128,128]{3,2,1,0:T(8,128)(2,1)} %param.6) | copy-start | bytes 1572868
  6.5 112.2 %all-gather.3.cloned.1.call-start = ((), (), s32[]{:S(2)}) async-start(), calls=%async_computation.1 | async-start | bytes 4718592 | tf_op jit(solution)/shard_map/all_gather | solution.py:56
  7.3 231.4 %reduce-scatter.2.cloned.1.call-start = ((), (), s32[]{:S(2)}) async-start(), calls=%async_computation.2 | async-start | bytes 2162688 | tf_op jit(solution)/shard_map/reduce_scatter | solution.py:62
  7.3 24.5 %collective-permute-start = (s32[16,1]{0,1:T(1,128)}, s32[16,1]{0,1:T(1,128)S(1)}, u32[]{:S(2)}, u32[]{:S(2)}) collective-permute-start(s32[16,1]{0,1:T(1,128)} %param.7), channel_id=1, source_target_pairs={{0,24},{8,32},{16,40},{24,48},{32,56},{40,64},{48,72},{56,80},{64,... | collective-permute-start | bytes 200 | tf_op jit(solution)/shard_map/ppermute | solution.py:15
  10.9 23.4 %collective-permute-start.1 = (s32[16,1]{0,1:T(1,128)}, s32[16,1]{0,1:T(1,128)S(1)}, u32[]{:S(2)}, u32[]{:S(2)}) collective-permute-start(s32[16,1]{0,1:T(1,128)} %param.7), channel_id=1, source_target_pairs={{0,16},{8,24},{16,32},{24,40},{32,48},{40,56},{48,64},{56,72},{64,... | collective-permute-start | bytes 200 | tf_op jit(solution)/shard_map/ppermute | solution.py:15
  11.3 26.1 %collective-permute-start.2 = (s32[16,1]{0,1:T(1,128)}, s32[16,1]{0,1:T(1,128)S(1)}, u32[]{:S(2)}, u32[]{:S(2)}) collective-permute-start(s32[16,1]{0,1:T(1,128)} %param.7), channel_id=1, source_target_pairs={{0,8},{8,16},{16,24},{24,32},{32,40},{40,48},{48,56},{56,64},{64,7... | collective-permute-start | bytes 200 | tf_op jit(solution)/shard_map/ppermute | solution.py:15
  11.6 26.2 %collective-permute-start.3 = (s32[16,1]{0,1:T(1,128)}, s32[16,1]{0,1:T(1,128)S(1)}, u32[]{:S(2)}, u32[]{:S(2)}) collective-permute-start(s32[16,1]{0,1:T(1,128)} %param.7), channel_id=1, source_target_pairs={{0,248},{8,0},{16,8},{24,16},{32,24},{40,32},{48,40},{56,48},{64,5... | collective-permute-start | bytes 200 | tf_op jit(solution)/shard_map/ppermute | solution.py:15
  11.8 34.5 %collective-permute-start.6 = (bf16[16,1,128,128]{3,2,1,0:T(8,128)(2,1)}, bf16[16,1,128,128]{3,2,1,0:T(8,128)(2,1)S(1)}, u32[]{:S(2)}, u32[]{:S(2)}) collective-permute-start(bf16[16,1,128,128]{3,2,1,0:T(8,128)(2,1)} %param.6), channel_id=1, source_target_pairs={{0,24},{8,32},{16,40},{24,48},{32,56},{40,64},{48,72},{56,80},{64,... | collective-permute-start | bytes 1572872 | tf_op jit(solution)/shard_map/ppermute | solution.py:15
  31.8 6.0 %collective-permute-start.4 = (s32[16,1]{0,1:T(1,128)}, s32[16,1]{0,1:T(1,128)S(1)}, u32[]{:S(2)}, u32[]{:S(2)}) collective-permute-start(s32[16,1]{0,1:T(1,128)} %param.7), channel_id=1, source_target_pairs={{0,240},{8,248},{16,0},{24,8},{32,16},{40,24},{48,32},{56,40},{64,... | collective-permute-start | bytes 200 | tf_op jit(solution)/shard_map/ppermute | solution.py:15
  34.3 4.7 %collective-permute-start.5 = (s32[16,1]{0,1:T(1,128)}, s32[16,1]{0,1:T(1,128)S(1)}, u32[]{:S(2)}, u32[]{:S(2)}) collective-permute-start(s32[16,1]{0,1:T(1,128)} %param.7), channel_id=1, source_target_pairs={{0,232},{8,240},{16,248},{24,0},{32,8},{40,16},{48,24},{56,32},{64... | collective-permute-start | bytes 200 | tf_op jit(solution)/shard_map/ppermute | solution.py:15
  37.3 16.9 %collective-permute-start.7 = (bf16[16,1,128,128]{3,2,1,0:T(8,128)(2,1)}, bf16[16,1,128,128]{3,2,1,0:T(8,128)(2,1)S(1)}, u32[]{:S(2)}, u32[]{:S(2)}) collective-permute-start(bf16[16,1,128,128]{3,2,1,0:T(8,128)(2,1)} %param.6), channel_id=1, source_target_pairs={{0,16},{8,24},{16,32},{24,40},{32,48},{40,56},{48,64},{56,72},{64,... | collective-permute-start | bytes 1572872 | tf_op jit(solution)/shard_map/ppermute | solution.py:15
  37.7 17.7 %collective-permute-start.8 = (bf16[16,1,128,128]{3,2,1,0:T(8,128)(2,1)}, bf16[16,1,128,128]{3,2,1,0:T(8,128)(2,1)S(1)}, u32[]{:S(2)}, u32[]{:S(2)}) collective-permute-start(bf16[16,1,128,128]{3,2,1,0:T(8,128)(2,1)} %param.6), channel_id=1, source_target_pairs={{0,8},{8,16},{16,24},{24,32},{32,40},{40,48},{48,56},{56,64},{64,7... | collective-permute-start | bytes 1572872 | tf_op jit(solution)/shard_map/ppermute | solution.py:15
  37.8 19.3 %collective-permute-start.9 = (bf16[16,1,128,128]{3,2,1,0:T(8,128)(2,1)}, bf16[16,1,128,128]{3,2,1,0:T(8,128)(2,1)S(1)}, u32[]{:S(2)}, u32[]{:S(2)}) collective-permute-start(bf16[16,1,128,128]{3,2,1,0:T(8,128)(2,1)} %param.6), channel_id=1, source_target_pairs={{0,248},{8,0},{16,8},{24,16},{32,24},{40,32},{48,40},{56,48},{64,5... | collective-permute-start | bytes 1572872 | tf_op jit(solution)/shard_map/ppermute | solution.py:15
  38.9 21.1 %collective-permute-start.10 = (bf16[16,1,128,128]{3,2,1,0:T(8,128)(2,1)}, bf16[16,1,128,128]{3,2,1,0:T(8,128)(2,1)S(1)}, u32[]{:S(2)}, u32[]{:S(2)}) collective-permute-start(bf16[16,1,128,128]{3,2,1,0:T(8,128)(2,1)} %param.6), channel_id=1, source_target_pairs={{0,240},{8,248},{16,0},{24,8},{32,16},{40,24},{48,32},{56,40},{64,... | collective-permute-start | bytes 1572872 | tf_op jit(solution)/shard_map/ppermute | solution.py:15
  46.3 24.9 %collective-permute-start.11 = (bf16[16,1,128,128]{3,2,1,0:T(8,128)(2,1)}, bf16[16,1,128,128]{3,2,1,0:T(8,128)(2,1)S(1)}, u32[]{:S(2)}, u32[]{:S(2)}) collective-permute-start(bf16[16,1,128,128]{3,2,1,0:T(8,128)(2,1)} %param.6), channel_id=1, source_target_pairs={{0,232},{8,240},{16,248},{24,0},{32,8},{40,16},{48,24},{56,32},{64... | collective-permute-start | bytes 1572872 | tf_op jit(solution)/shard_map/ppermute | solution.py:15
Sparse Core Ops, SparseCore 0:
  9.2 57.7 all-gather.2
  148.1 90.4 reduce-scatter.1
where the time goes:
time: 249 us; the launch traced here: 246 us
  waiting for transfers between devices  111 us (45%)
  local copies, waits for them, and re-layouts  50.7 us (20%)
  other arithmetic  19 us (8%)
  starting transfers between devices  17.8 us (7%)
  matrix products  17.1 us (7%)
  blocking collectives  16.5 us (7%)
  between operations  13.5 us (5%)
    reduce_scatter x1, waiting for transfers between devices, body(): lax.psum_scatter(summed.reshape(flat_rows.shape[2] // row_devices * lax.a...  90.6 us
    ppermute x12, waiting for transfers between devices, from_behind(): return lax.ppermute(value, axis, pairs)  19.5 us
    ppermute x12, starting transfers between devices, from_behind(): return lax.ppermute(value, axis, pairs)  17.8 us
    all_gather x1, blocking collectives, body(): lax.all_gather(zcol, 'cols', axis=1, tiled=True)  16.5 us
    select_n x1, local copies, waits for them, and re-layouts, body(): chosen = jnp.take(fetched, position.reshape(-1), axis=0)  13.8 us
    gather x1, local copies, waits for them, and re-layouts, body(): chosen = jnp.take(fetched, position.reshape(-1), axis=0)  12.7 us
    select_n x1, other arithmetic, body(): chosen = jnp.take(fetched, position.reshape(-1), axis=0)  10.2 us
    dot_general x1, matrix products, body(): jnp.einsum('rkab,rkcbe->rcae', fblocks, expanded, preferred_element_type=...  9.98 us
  transfers between devices with their start and end apart: 14, of which 6 were waited for; matrix products, arithmetic and copies ran while one was open for 23% of the time, Pallas kernels for 0%

commit v1 on v0

v1 whole, which is shorter than its diff:
```python
import jax
import jax.numpy as jnp
from jax import lax
from jax.experimental import pallas as pl
from jax.experimental.pallas import tpu as pltpu
from jax.sharding import PartitionSpec as P

B = 128
K = 20
CB = 2
ROWS = 16
CHIPS = 16
GROUPS = 8
NB = 512
SLOTS = 7
OWN = 3
HALF = ROWS // 2
WIDE = CB * B
OUT = 64
ORDER = (0, -1, 1, -2, 2, -3, 3, 4)
MESH = pl.DeviceIdType.MESH
F32 = jnp.float32
BF16 = jnp.bfloat16


def kernel(
    fcol_hbm,
    zcol_hbm,
    f_hbm,
    z_hbm,
    out,
    fv,
    halo,
    zexp,
    ring,
    tags,
    wide,
    turned,
    masks,
    part,
    other,
    chip_sum,
    arrived,
    total,
    fcol,
    zcol,
    small_sem,
    z_sem,
    f_sem,
    halo_send,
    halo_recv,
    ring_send,
    ring_recv,
    tag_send,
    tag_recv,
    pair_send,
    pair_recv,
    sum_send,
    sum_recv,
):
    r = lax.axis_index("rows")
    z = lax.axis_index("cols")
    m = lax.div(r, 2)
    q = lax.rem(r, 2)
    s = 2 * q - 1

    def chip(step):
        return lax.rem(m + step + 2 * CHIPS, CHIPS)

    def group(step):
        return lax.rem(z + step + 2 * GROUPS, GROUPS)

    sibling = (r - s, z)

    load_z = []
    for half in range(2):
        load_z.append(
            pltpu.make_async_copy(
                z_hbm.at[pl.ds(half * HALF * B, HALF * B)],
                halo.at[OWN, half, pl.ds(0, HALF * B)],
                z_sem.at[half],
            )
        )
        load_z[-1].start()
    load_zcol = pltpu.make_async_copy(zcol_hbm, zcol, small_sem.at[0])
    load_zcol.start()
    load_fcol = pltpu.make_async_copy(fcol_hbm, fcol, small_sem.at[1])
    load_fcol.start()
    load_f = []
    for g in range(4):
        rows = pl.ds(4 * g, 4)
        load_f.append(pltpu.make_async_copy(f_hbm.at[rows], fv.at[rows], f_sem.at[g]))
        load_f[-1].start()

    barrier = pltpu.get_barrier_semaphore()
    peers = [(r, group(1)), (r, group(-1)), sibling, (2 * chip(s) + 1 - q, z)]
    peers += [(2 * chip(j) + q, z) for j in range(1, CHIPS)]
    for peer in peers:
        pl.semaphore_signal(barrier, inc=1, device_id=peer, device_id_type=MESH)

    def remote(src, dst, send, recv, device):
        return pltpu.make_async_remote_copy(
            src_ref=src, dst_ref=dst, send_sem=send, recv_sem=recv,
            device_id=device, device_id_type=MESH,
        )

    sent = []

    def go(copy):
        copy.start()
        sent.append(copy)

    def drain(count):
        for copy in sent[:count]:
            copy.wait_send()
        del sent[:count]

    def ring_copy(sense, distance, half):
        n = group(-sense * (distance - 1))
        at = (0 if sense == 1 else 1, distance - 1, half)
        if distance == 1:
            source = z_hbm.at[pl.ds(half * HALF * B, HALF * B)]
        else:
            source = ring.at[n, half]
        return remote(
            source, ring.at[n, half], ring_send.at[at], ring_recv.at[at], (r, group(sense))
        )

    def ring_wait(sense, distance, half):
        n = group(-sense * distance)
        at = (0 if sense == 1 else 1, distance - 1, half)
        remote(
            ring.at[n, half], ring.at[n, half], ring_send.at[at], ring_recv.at[at],
            (r, group(sense)),
        ).wait_recv()

    def tag_copy(sense, distance):
        n = group(-sense * (distance - 1))
        at = (0 if sense == 1 else 1, distance - 1)
        return remote(
            tags.at[n], tags.at[n], tag_send.at[at], tag_recv.at[at], (r, group(sense))
        )

    def tag_wait(sense, distance):
        n = group(-sense * distance)
        at = (0 if sense == 1 else 1, distance - 1)
        remote(
            tags.at[n], tags.at[n], tag_send.at[at], tag_recv.at[at], (r, group(sense))
        ).wait_recv()

    pl.semaphore_wait(barrier, len(peers))
    go(ring_copy(1, 1, 0))
    go(ring_copy(-1, 1, 1))

    load_zcol.wait()
    load_fcol.wait()
    row_of = lax.broadcasted_iota(jnp.int32, (ROWS, B), 0)

    def mask_tile(first):
        tile = jnp.zeros((ROWS, B), F32)
        for i in range(first, ROWS):
            tile = jnp.where(row_of == i - first, zcol[0, i].astype(F32), tile)
        return tile.astype(BF16)

    tags[z] = mask_tile(0)
    halo[OWN, 0, pl.ds(HALF * B, ROWS)] = mask_tile(0)
    halo[OWN, 1, pl.ds(HALF * B, ROWS)] = mask_tile(HALF)
    for half in range(2):
        load_z[half].wait()

    def halo_copy(step, order, src_slot, dst_slot, device, core=q):
        half = core if order == 0 else 1 - core
        return remote(
            halo.at[src_slot, half], halo.at[dst_slot, half],
            halo_send.at[step, order], halo_recv.at[step, order], device,
        )

    def halo_wait(step, order, slot):
        halo_copy(step, order, slot, slot, sibling, q if step < 2 else 1 - q).wait_recv()

    for order in range(2):
        go(halo_copy(0, order, OWN, 1, (2 * chip(1) + q, z)))
        go(halo_copy(1, order, OWN, 5, (2 * chip(-1) + q, z)))
    for order in range(2):
        go(halo_copy(2, order, OWN, 3 + s, sibling))
    go(ring_copy(1, 1, 1))
    go(ring_copy(-1, 1, 0))
    go(tag_copy(1, 1))
    go(tag_copy(-1, 1))

    def expand_slot(slot, half):
        masks[...] = halo[slot, half, pl.ds(HALF * B, ROWS)].astype(F32)

        @pl.loop(0, HALF)
        def _(j):
            block = halo[slot, half, pl.ds(pl.multiple_of(j * B, B), B)].astype(F32)
            second = masks[pl.ds(j, 1), :]
            at = slot * ROWS + half * HALF + j
            zexp[at, :, 0:B] = (block * (1.0 - second)).astype(BF16)
            zexp[at, :, B:WIDE] = (block * second).astype(BF16)

    def expand_both(slot):
        expand_slot(slot, 0)
        expand_slot(slot, 1)

    expand_both(OWN)
    halo_wait(2, 0, 3 - s)
    halo_wait(2, 1, 3 - s)
    expand_both(3 - s)

    def expand_half(t, half):
        n = group(ORDER[t])
        masks[...] = tags[n].astype(F32)

        @pl.loop(0, HALF)
        def _(j):
            block = ring[n, half, pl.ds(pl.multiple_of(j * B, B), B)].astype(F32)
            second = masks[pl.ds(half * HALF + j, 1), :]
            rows = pl.ds(pl.multiple_of((half * HALF + j) * B, B), B)
            wide[t, rows, 0:B] = (block * (1.0 - second)).astype(BF16)
            wide[t, rows, B:WIDE] = (block * second).astype(BF16)

    def forward(distance, first):
        right, left = (0, 1) if first else (1, 0)
        for sense, half in ((1, right), (-1, left)):
            ring_wait(sense, distance, half)
            if distance < 3 or (distance == 3 and first):
                go(ring_copy(sense, distance + 1, half))
            if first:
                tag_wait(sense, distance)
                if distance < 3 or sense == 1:
                    go(tag_copy(sense, distance + 1))
        expand_half(2 * distance - 1, right)
        expand_half(2 * distance, left)

    def halo_forward(order):
        halo_wait(0, order, 1)
        halo_wait(1, order, 5)
        go(halo_copy(5, order, 3 - 2 * s, 3 - 3 * s, (2 * chip(s) + 1 - q, z)))
        go(halo_copy(3, order, 1, 1 + s, sibling))
        go(halo_copy(4, order, 5, 5 + s, sibling))

    forward(1, True)
    halo_forward(0)
    forward(1, False)
    halo_forward(1)
    expand_both(1)
    expand_both(5)
    for order in range(2):
        halo_wait(3, order, 1 - s)
        halo_wait(4, order, 5 - s)
    expand_both(1 - s)
    expand_both(5 - s)

    first_row = (r - OWN) * ROWS

    def place(column):
        return jnp.minimum(lax.rem(column - first_row + NB, NB), SLOTS * ROWS - 1)

    def product_row(i):
        left = jnp.concatenate([fv[i, pl.ds(k * B, B)] for k in range(K)], axis=1)
        right = jnp.concatenate([zexp[place(fcol[i, k])] for k in range(K)], axis=0)
        acc = jnp.dot(left, right, preferred_element_type=F32)
        rows = pl.ds(pl.multiple_of(i * B, B), B)
        for c in range(CB):
            turned[c * B:(c + 1) * B, rows] = jnp.transpose(acc[:, c * B:(c + 1) * B]).astype(BF16)

    def product_rows(first):
        for i in range(4):
            product_row(first + i)

    for g in range(4):
        load_f[g].wait()
    near = HALF * (1 - q)
    halo_wait(5, 0, 3 + 3 * s)
    expand_slot(3 + 3 * s, 1 - q)
    product_rows(near)
    forward(2, True)
    product_rows(near + 4)
    halo_wait(5, 1, 3 + 3 * s)
    expand_slot(3 + 3 * s, q)
    product_rows(HALF * q)
    forward(2, False)
    product_rows(HALF * q + 4)

    def group_of(t):
        return group(ORDER[t])

    pair_copies = []

    def window(t):
        right = wide[t]
        if t == 0:
            right = zexp[OWN * ROWS:(OWN + 1) * ROWS].reshape(ROWS * B, WIDE)
        product = jnp.transpose(jnp.dot(turned[...], right, preferred_element_type=F32))
        for b in range(4):
            part[t, b % 2, b // 2] = product[b * OUT:(b + 1) * OUT]
        copy = remote(
            part.at[t, 1 - q], other.at[t], pair_send.at[t], pair_recv.at[t], sibling
        )
        pair_copies.append(copy)
        go(copy)

    def sum_copy(t, h):
        d = 2 * group_of(t) + h
        return d, remote(
            chip_sum.at[t, h], arrived.at[m], sum_send.at[t, h], sum_recv.at[m],
            (2 * d + q, z),
        )

    def finish(t):
        pair_copies[t].wait_recv()
        for h in range(2):
            both = part[t, q, h] + other[t, h]
            chip_sum[t, h] = both.astype(BF16)
            d, copy = sum_copy(t, h)

            @pl.when(d == m)
            def _():
                total[...] = both

            @pl.when(d != m)
            def _():
                copy.start()

    window(0)
    window(1)
    finish(0)
    window(2)
    finish(1)
    early = len(sent)
    forward(3, True)
    window(3)
    finish(2)
    window(4)
    finish(3)
    finish(4)
    forward(3, False)
    window(5)
    window(6)
    finish(5)
    finish(6)
    drain(early)
    tag_wait(1, 4)
    ring_wait(1, 4, 0)
    ring_wait(-1, 4, 1)
    expand_half(7, 0)
    expand_half(7, 1)
    window(7)
    finish(7)

    acc = total[...]
    for j in range(1, CHIPS):
        source = chip(j)
        remote(
            arrived.at[source], arrived.at[source], sum_send.at[0, 0], sum_recv.at[source], sibling
        ).wait_recv()
        acc += arrived[source].astype(F32)
    out[...] = acc

    drain(len(sent))
    for t in range(GROUPS):
        for h in range(2):
            d, copy = sum_copy(t, h)

            @pl.when(d != m)
            def _():
                copy.wait_send()


def body(fblocks, fcol, zblocks, zcol):
    dma = pltpu.SemaphoreType.DMA
    return pl.pallas_call(
        kernel,
        out_shape=jax.ShapeDtypeStruct((OUT, WIDE), F32),
        in_specs=[pl.BlockSpec(memory_space=pl.ANY)] * 4,
        out_specs=pl.BlockSpec(memory_space=pltpu.VMEM),
        scratch_shapes=[
            pltpu.VMEM((ROWS, K * B, B), BF16),
            pltpu.VMEM((SLOTS, 2, HALF * B + ROWS, B), BF16),
            pltpu.VMEM((SLOTS * ROWS, B, WIDE), BF16),
            pltpu.VMEM((GROUPS, 2, HALF * B, B), BF16),
            pltpu.VMEM((GROUPS, ROWS, B), BF16),
            pltpu.VMEM((GROUPS, ROWS * B, WIDE), BF16),
            pltpu.VMEM((WIDE, ROWS * B), BF16),
            pltpu.VMEM((ROWS, B), F32),
            pltpu.VMEM((GROUPS, 2, 2, OUT, WIDE), F32),
            pltpu.VMEM((GROUPS, 2, OUT, WIDE), F32),
            pltpu.VMEM((GROUPS, 2, OUT, WIDE), BF16),
            pltpu.VMEM((CHIPS, OUT, WIDE), BF16),
            pltpu.VMEM((OUT, WIDE), F32),
            pltpu.SMEM((ROWS, K), jnp.int32),
            pltpu.SMEM((1, ROWS), jnp.int32),
            dma((2,)),
            dma((2,)),
            dma((4,)),
            dma((6, 2)),
            dma((6, 2)),
            dma((2, 4, 2)),
            dma((2, 4, 2)),
            dma((2, 4)),
            dma((2, 4)),
            dma((GROUPS,)),
            dma((GROUPS,)),
            dma((GROUPS, 2)),
            dma((CHIPS,)),
        ],
        compiler_params=pltpu.CompilerParams(
            collective_id=0, has_side_effects=True, vmem_limit_bytes=60 * 2**20
        ),
    )(
        fcol,
        zcol.reshape(1, ROWS),
        fblocks.reshape(ROWS, K * B, B),
        zblocks.reshape(ROWS * B, B),
    )


def solution(mesh):
    in_specs = (
        P("rows", None, None, None),
        P("rows", None),
        P("rows", "cols", None, None),
        P("rows", "cols"),
    )
    out_specs = P("rows", "cols")
    return jax.shard_map(body, mesh=mesh, in_specs=in_specs, out_specs=out_specs, check_vma=False)
```

time: 249 us -> 63.3 us (0.25); the launches traced: 246 us -> 63.1 us
  waiting for transfers between devices: 111 us -> 0 us
  Pallas kernels: 0 us -> 61.7 us
  local copies, waits for them, and re-layouts: 50.7 us -> 1.47 us
  other arithmetic: 19 us -> 0 us
  starting transfers between devices: 17.8 us -> 0 us
  matrix products: 17.1 us -> 0 us
  blocking collectives: 16.5 us -> 0 us
  between operations: 13.5 us -> 0.01 us
    reduce_scatter x1 -> x0, waiting for transfers between devices: 90.6 us -> none  [body(): lax.psum_scatter(summed.reshape(flat_rows.shape[2] // row_devices * lax.a...]
    pallas_call x0 -> x1, Pallas kernels: none -> 61.7 us  [body(): pl.pallas_call(kernel, out_shape=jax.ShapeDtypeStruct((OUT, WIDE), F32),...]
    ppermute x12 -> x0, waiting for transfers between devices: 19.5 us -> none  [from_behind(): return lax.ppermute(value, axis, pairs)]
    select_n x5 -> x0, other arithmetic: 18.9 us -> none  [the longest x1 10.2 us: body(): chosen = jnp.take(fetched, position.reshape(-1), axis=0)]
    ppermute x12 -> x0, starting transfers between devices: 17.8 us -> none  [from_behind(): return lax.ppermute(value, axis, pairs)]
    dot_general x2 -> x0, matrix products: 17.1 us -> none  [the longest x1 9.98 us: body(): jnp.einsum('rkab,rkcbe->rcae', fblocks, expanded, preferred_element_type=...]
    all_gather x1 -> x0, blocking collectives: 16.5 us -> none  [body(): lax.all_gather(zcol, 'cols', axis=1, tiled=True)]
    gather x3 -> x0, local copies, waits for them, and re-layouts: 15.2 us -> none  [the longest x1 12.7 us: body(): chosen = jnp.take(fetched, position.reshape(-1), axis=0)]
  transfers between devices with their start and end apart: 14 -> 0, of which waited for: 6 -> 0; matrix products, arithmetic and copies ran while one was open for 23% -> 0% of each run, Pallas kernels for 0% -> 0%
where the time goes in v1:
time: 63.3 us; the launch traced here: 63.1 us
  Pallas kernels  61.7 us (97%)
  local copies, waits for them, and re-layouts  1.47 us (2%)
    pallas_call x1, Pallas kernels, body(): pl.pallas_call(kernel, out_shape=jax.ShapeDtypeStruct((OUT, WIDE), F32),...  61.7 us
    unnamed x1, local copies, waits for them, and re-layouts  1.47 us

profile of v1, /device:TPU:5, one launch (start us, length us, event | category | flops | bytes accessed | tf_op | source)
XLA Modules:
  0.0 63.1 jit_solution(7629084322823981530)
XLA Ops:
  0.0 61.7 %shard_map.46 = f32[64,256]{1,0:T(8,128)} custom-call(s32[16,20]{1,0:T(8,128)} %fcol_hbm.1, s32[1,16]{1,0:T(1,128)} %bitcast.5, bf16[16,2560,128]{2,1,0:T(8,128)(2,1)} %bitcast.3, bf16[2048,128]{1,0:T(8,128)(2,1)} %bitcast.4), custom_call_target="tpu_custom_call" | custom-call | tf_op jit(solution)/shard_map/pallas_call | solution.py:373
  61.7 1.5 %copy.6 = f32[64,256]{1,0:T(8,128)} copy(f32[64,256]{1,0:T(8,128)} %shard_map.46) | data formatting | bytes 131072

commit v2 on v1

--- a/solution.py
+++ b/solution.py
@@ -282,6 +282,8 @@
     product_rows(HALF * q)
     forward(2, False)
     product_rows(HALF * q + 4)
+    early = len(sent)
+    forward(3, True)
 
     def group_of(t):
         return group(ORDER[t])
@@ -325,21 +327,17 @@
 
     window(0)
     window(1)
+    window(2)
     finish(0)
-    window(2)
+    window(3)
     finish(1)
-    early = len(sent)
-    forward(3, True)
-    window(3)
+    window(4)
     finish(2)
-    window(4)
-    finish(3)
-    finish(4)
     forward(3, False)
     window(5)
+    finish(3)
     window(6)
-    finish(5)
-    finish(6)
+    finish(4)
     drain(early)
     tag_wait(1, 4)
     ring_wait(1, 4, 0)
@@ -347,6 +345,8 @@
     expand_half(7, 0)
     expand_half(7, 1)
     window(7)
+    finish(5)
+    finish(6)
     finish(7)
 
     acc = total[...]

time: 63.3 us -> 64 us (1.011)
  no operation moved by 1% of the time
where the time goes in v2:
time: 64 us; the launch traced here: 63.8 us
  Pallas kernels  62.3 us (97%)
  local copies, waits for them, and re-layouts  1.47 us (2%)
    pallas_call x1, Pallas kernels, body(): pl.pallas_call(kernel, out_shape=jax.ShapeDtypeStruct((OUT, WIDE), F32),...  62.3 us
    unnamed x1, local copies, waits for them, and re-layouts  1.47 us

profile of v2, /device:TPU:5, one launch (start us, length us, event | category | flops | bytes accessed | tf_op | source)
XLA Modules:
  0.0 63.8 jit_solution(8008439676607360475)
XLA Ops:
  0.0 62.3 %shard_map.46 = f32[64,256]{1,0:T(8,128)} custom-call(s32[16,20]{1,0:T(8,128)} %fcol_hbm.1, s32[1,16]{1,0:T(1,128)} %bitcast.5, bf16[16,2560,128]{2,1,0:T(8,128)(2,1)} %bitcast.3, bf16[2048,128]{1,0:T(8,128)(2,1)} %bitcast.4), custom_call_target="tpu_custom_call" | custom-call | tf_op jit(solution)/shard_map/pallas_call | solution.py:373
  62.3 1.5 %copy.6 = f32[64,256]{1,0:T(8,128)} copy(f32[64,256]{1,0:T(8,128)} %shard_map.46) | data formatting | bytes 131072

commit v3 on v1

--- a/solution.py
+++ b/solution.py
@@ -17,6 +17,8 @@
 HALF = ROWS // 2
 WIDE = CB * B
 OUT = 64
+SUB = 4
+LAST = GROUPS - 1
 ORDER = (0, -1, 1, -2, 2, -3, 3, 4)
 MESH = pl.DeviceIdType.MESH
 F32 = jnp.float32
@@ -57,6 +59,8 @@
     pair_recv,
     sum_send,
     sum_recv,
+    last_send,
+    last_recv,
 ):
     r = lax.axis_index("rows")
     z = lax.axis_index("cols")
@@ -134,6 +138,16 @@
             (r, group(sense)),
         ).wait_recv()
 
+    def last_copy(sense, sub, distance=3):
+        n = group(-sense * distance)
+        half = 0 if sense == 1 else 1
+        at = (half, sub)
+        part_of = ring.at[n, half, pl.ds(sub * SUB * B, SUB * B)]
+        return remote(part_of, part_of, last_send.at[at], last_recv.at[at], (r, group(sense)))
+
+    def last_wait(sense, sub):
+        last_copy(sense, sub, 4).wait_recv()
+
     def tag_copy(sense, distance):
         n = group(-sense * (distance - 1))
         at = (0 if sense == 1 else 1, distance - 1)
@@ -193,11 +207,11 @@
 
         @pl.loop(0, HALF)
         def _(j):
-            block = halo[slot, half, pl.ds(pl.multiple_of(j * B, B), B)].astype(F32)
-            second = masks[pl.ds(j, 1), :]
+            block = halo[slot, half, pl.ds(pl.multiple_of(j * B, B), B)]
+            second = masks[pl.ds(j, 1), :].astype(BF16)
             at = slot * ROWS + half * HALF + j
-            zexp[at, :, 0:B] = (block * (1.0 - second)).astype(BF16)
-            zexp[at, :, B:WIDE] = (block * second).astype(BF16)
+            zexp[at, :, 0:B] = block * (1 - second)
+            zexp[at, :, B:WIDE] = block * second
 
     def expand_both(slot):
         expand_slot(slot, 0)
@@ -208,24 +222,27 @@
     halo_wait(2, 1, 3 - s)
     expand_both(3 - s)
 
-    def expand_half(t, half):
+    def expand_half(t, half, first=0, last=HALF):
         n = group(ORDER[t])
         masks[...] = tags[n].astype(F32)
 
-        @pl.loop(0, HALF)
+        @pl.loop(first, last)
         def _(j):
-            block = ring[n, half, pl.ds(pl.multiple_of(j * B, B), B)].astype(F32)
-            second = masks[pl.ds(half * HALF + j, 1), :]
+            block = ring[n, half, pl.ds(pl.multiple_of(j * B, B), B)]
+            second = masks[pl.ds(half * HALF + j, 1), :].astype(BF16)
             rows = pl.ds(pl.multiple_of((half * HALF + j) * B, B), B)
-            wide[t, rows, 0:B] = (block * (1.0 - second)).astype(BF16)
-            wide[t, rows, B:WIDE] = (block * second).astype(BF16)
+            wide[t, rows, 0:B] = block * (1 - second)
+            wide[t, rows, B:WIDE] = block * second
 
     def forward(distance, first):
         right, left = (0, 1) if first else (1, 0)
         for sense, half in ((1, right), (-1, left)):
             ring_wait(sense, distance, half)
-            if distance < 3 or (distance == 3 and first):
+            if distance < 3:
                 go(ring_copy(sense, distance + 1, half))
+            elif first:
+                for sub in range(2):
+                    go(last_copy(sense, sub))
             if first:
                 tag_wait(sense, distance)
                 if distance < 3 or sense == 1:
@@ -263,7 +280,7 @@
         acc = jnp.dot(left, right, preferred_element_type=F32)
         rows = pl.ds(pl.multiple_of(i * B, B), B)
         for c in range(CB):
-            turned[c * B:(c + 1) * B, rows] = jnp.transpose(acc[:, c * B:(c + 1) * B]).astype(BF16)
+            turned[c * B:(c + 1) * B, rows] = jnp.transpose(acc[:, c * B:(c + 1) * B].astype(BF16))
 
     def product_rows(first):
         for i in range(4):
@@ -288,11 +305,25 @@
 
     pair_copies = []
 
+    def last_product():
+        acc = jnp.zeros((WIDE, WIDE), F32)
+        for sub in range(2):
+            for sense, half in ((1, 0), (-1, 1)):
+                last_wait(sense, sub)
+                expand_half(LAST, half, sub * SUB, (sub + 1) * SUB)
+                rows = pl.ds((half * HALF + sub * SUB) * B, SUB * B)
+                acc += jnp.dot(turned[:, rows], wide[LAST, rows], preferred_element_type=F32)
+        return acc
+
     def window(t):
-        right = wide[t]
-        if t == 0:
-            right = zexp[OWN * ROWS:(OWN + 1) * ROWS].reshape(ROWS * B, WIDE)
-        product = jnp.transpose(jnp.dot(turned[...], right, preferred_element_type=F32))
+        if t == LAST:
+            product = last_product()
+        else:
+            right = wide[t]
+            if t == 0:
+                right = zexp[OWN * ROWS:(OWN + 1) * ROWS].reshape(ROWS * B, WIDE)
+            product = jnp.dot(turned[...], right, preferred_element_type=F32)
+        product = jnp.transpose(product)
         for b in range(4):
             part[t, b % 2, b // 2] = product[b * OUT:(b + 1) * OUT]
         copy = remote(
@@ -324,12 +355,12 @@
                 copy.start()
 
     window(0)
+    early = len(sent)
+    forward(3, True)
     window(1)
     finish(0)
     window(2)
     finish(1)
-    early = len(sent)
-    forward(3, True)
     window(3)
     finish(2)
     window(4)
@@ -342,10 +373,6 @@
     finish(6)
     drain(early)
     tag_wait(1, 4)
-    ring_wait(1, 4, 0)
-    ring_wait(-1, 4, 1)
-    expand_half(7, 0)
-    expand_half(7, 1)
     window(7)
     finish(7)
 
@@ -404,6 +431,8 @@
             dma((GROUPS,)),
             dma((GROUPS, 2)),
             dma((CHIPS,)),
+            dma((2, 2)),
+            dma((2, 2)),
         ],
         compiler_params=pltpu.CompilerParams(
             collective_id=0, has_side_effects=True, vmem_limit_bytes=60 * 2**20

time: 63.3 us -> 63.5 us (level)
  no operation moved by 1% of the time
where the time goes in v3:
time: 63.5 us; the launch traced here: 63.4 us
  Pallas kernels  61.9 us (97%)
  local copies, waits for them, and re-layouts  1.47 us (2%)
    pallas_call x1, Pallas kernels, body(): pl.pallas_call(kernel, out_shape=jax.ShapeDtypeStruct((OUT, WIDE), F32),...  61.9 us
    unnamed x1, local copies, waits for them, and re-layouts  1.47 us

profile of v3, /device:TPU:5, one launch (start us, length us, event | category | flops | bytes accessed | tf_op | source)
XLA Modules:
  0.0 63.4 jit_solution(15278745130889237415)
XLA Ops:
  0.0 61.9 %shard_map.46 = f32[64,256]{1,0:T(8,128)} custom-call(s32[16,20]{1,0:T(8,128)} %fcol_hbm.1, s32[1,16]{1,0:T(1,128)} %bitcast.5, bf16[16,2560,128]{2,1,0:T(8,128)(2,1)} %bitcast.3, bf16[2048,128]{1,0:T(8,128)(2,1)} %bitcast.4), custom_call_target="tpu_custom_call" | custom-call | tf_op jit(solution)/shard_map/pallas_call | solution.py:400
  61.9 1.5 %copy.6 = f32[64,256]{1,0:T(8,128)} copy(f32[64,256]{1,0:T(8,128)} %shard_map.46) | data formatting | bytes 131072

commit v4 on v3

--- a/solution.py
+++ b/solution.py
@@ -399,7 +399,7 @@
     dma = pltpu.SemaphoreType.DMA
     return pl.pallas_call(
         kernel,
-        out_shape=jax.ShapeDtypeStruct((OUT, WIDE), F32),
+        out_shape=pltpu.VMEM((OUT, WIDE), F32),
         in_specs=[pl.BlockSpec(memory_space=pl.ANY)] * 4,
         out_specs=pl.BlockSpec(memory_space=pltpu.VMEM),
         scratch_shapes=[

time: 63.5 us -> 62 us (0.976)
  local copies, waits for them, and re-layouts: 1.47 us -> 0.63 us
    unnamed x1, local copies, waits for them, and re-layouts: 1.47 us -> 0.63 us
where the time goes in v4:
time: 62 us; the launch traced here: 61.9 us
  Pallas kernels  61.3 us (99%)
  local copies, waits for them, and re-layouts  0.63 us (1%)
    pallas_call x1, Pallas kernels, body(): pl.pallas_call(kernel, out_shape=pltpu.VMEM((OUT, WIDE), F32), in_specs=[...  61.3 us

profile of v4, /device:TPU:5, one launch (start us, length us, event | category | flops | bytes accessed | tf_op | source)
XLA Modules:
  0.0 61.9 jit_solution(2212872367109538041)
XLA Ops:
  0.0 61.3 %shard_map.46 = f32[64,256]{1,0:T(8,128)S(1)} custom-call(s32[16,20]{1,0:T(8,128)} %fcol_hbm.1, s32[1,16]{1,0:T(1,128)} %bitcast.5, bf16[16,2560,128]{2,1,0:T(8,128)(2,1)} %bitcast.3, bf16[2048,128]{1,0:T(8,128)(2,1)} %bitcast.4), custom_call_target="tpu_custom_call" | custom-call | tf_op jit(solution)/shard_map/pallas_call | solution.py:400
  61.3 0.6 %copy.6 = f32[64,256]{1,0:T(8,128)} copy(f32[64,256]{1,0:T(8,128)S(1)} %shard_map.46) | data formatting | bytes 131072

commit v5 on v4

--- a/solution.py
+++ b/solution.py
@@ -17,7 +17,8 @@
 HALF = ROWS // 2
 WIDE = CB * B
 OUT = 64
-SUB = 4
+CHUNKS = 4
+CHUNK = ROWS // CHUNKS
 LAST = GROUPS - 1
 ORDER = (0, -1, 1, -2, 2, -3, 3, 4)
 MESH = pl.DeviceIdType.MESH
@@ -59,8 +60,6 @@
     pair_recv,
     sum_send,
     sum_recv,
-    last_send,
-    last_recv,
 ):
     r = lax.axis_index("rows")
     z = lax.axis_index("cols")
@@ -119,34 +118,24 @@
             copy.wait_send()
         del sent[:count]
 
-    def ring_copy(sense, distance, half):
+    def ring_copy(sense, distance, chunk):
         n = group(-sense * (distance - 1))
-        at = (0 if sense == 1 else 1, distance - 1, half)
+        at = (0 if sense == 1 else 1, distance - 1, chunk)
         if distance == 1:
-            source = z_hbm.at[pl.ds(half * HALF * B, HALF * B)]
+            source = z_hbm.at[pl.ds(chunk * CHUNK * B, CHUNK * B)]
         else:
-            source = ring.at[n, half]
+            source = ring.at[n, chunk]
         return remote(
-            source, ring.at[n, half], ring_send.at[at], ring_recv.at[at], (r, group(sense))
-        )
-
-    def ring_wait(sense, distance, half):
+            source, ring.at[n, chunk], ring_send.at[at], ring_recv.at[at], (r, group(sense))
+        )
+
+    def ring_wait(sense, distance, chunk):
         n = group(-sense * distance)
-        at = (0 if sense == 1 else 1, distance - 1, half)
+        at = (0 if sense == 1 else 1, distance - 1, chunk)
         remote(
-            ring.at[n, half], ring.at[n, half], ring_send.at[at], ring_recv.at[at],
+            ring.at[n, chunk], ring.at[n, chunk], ring_send.at[at], ring_recv.at[at],
             (r, group(sense)),
         ).wait_recv()
-
-    def last_copy(sense, sub, distance=3):
-        n = group(-sense * distance)
-        half = 0 if sense == 1 else 1
-        at = (half, sub)
-        part_of = ring.at[n, half, pl.ds(sub * SUB * B, SUB * B)]
-        return remote(part_of, part_of, last_send.at[at], last_recv.at[at], (r, group(sense)))
-
-    def last_wait(sense, sub):
-        last_copy(sense, sub, 4).wait_recv()
 
     def tag_copy(sense, distance):
         n = group(-sense * (distance - 1))
@@ -164,7 +153,7 @@
 
     pl.semaphore_wait(barrier, len(peers))
     go(ring_copy(1, 1, 0))
-    go(ring_copy(-1, 1, 1))
+    go(ring_copy(-1, 1, CHUNKS - 1))
 
     load_zcol.wait()
     load_fcol.wait()
@@ -177,6 +166,8 @@
         return tile.astype(BF16)
 
     tags[z] = mask_tile(0)
+    go(tag_copy(1, 1))
+    go(tag_copy(-1, 1))
     halo[OWN, 0, pl.ds(HALF * B, ROWS)] = mask_tile(0)
     halo[OWN, 1, pl.ds(HALF * B, ROWS)] = mask_tile(HALF)
     for half in range(2):
@@ -197,10 +188,9 @@
         go(halo_copy(1, order, OWN, 5, (2 * chip(-1) + q, z)))
     for order in range(2):
         go(halo_copy(2, order, OWN, 3 + s, sibling))
-    go(ring_copy(1, 1, 1))
-    go(ring_copy(-1, 1, 0))
-    go(tag_copy(1, 1))
-    go(tag_copy(-1, 1))
+    for j in range(1, CHUNKS):
+        go(ring_copy(1, 1, j))
+        go(ring_copy(-1, 1, CHUNKS - 1 - j))
 
     def expand_slot(slot, half):
         masks[...] = halo[slot, half, pl.ds(HALF * B, ROWS)].astype(F32)
@@ -222,33 +212,31 @@
     halo_wait(2, 1, 3 - s)
     expand_both(3 - s)
 
-    def expand_half(t, half, first=0, last=HALF):
+    def expand_chunk(t, chunk):
         n = group(ORDER[t])
         masks[...] = tags[n].astype(F32)
 
-        @pl.loop(first, last)
+        @pl.loop(0, CHUNK)
         def _(j):
-            block = ring[n, half, pl.ds(pl.multiple_of(j * B, B), B)]
-            second = masks[pl.ds(half * HALF + j, 1), :].astype(BF16)
-            rows = pl.ds(pl.multiple_of((half * HALF + j) * B, B), B)
+            block = ring[n, chunk, pl.ds(pl.multiple_of(j * B, B), B)]
+            second = masks[pl.ds(chunk * CHUNK + j, 1), :].astype(BF16)
+            rows = pl.ds(pl.multiple_of((chunk * CHUNK + j) * B, B), B)
             wide[t, rows, 0:B] = block * (1 - second)
             wide[t, rows, B:WIDE] = block * second
 
-    def forward(distance, first):
-        right, left = (0, 1) if first else (1, 0)
-        for sense, half in ((1, right), (-1, left)):
-            ring_wait(sense, distance, half)
-            if distance < 3:
-                go(ring_copy(sense, distance + 1, half))
-            elif first:
-                for sub in range(2):
-                    go(last_copy(sense, sub))
-            if first:
+    def forward(distance, j):
+        both = ((1, j), (-1, CHUNKS - 1 - j))
+        for sense, chunk in both:
+            ring_wait(sense, distance, chunk)
+            if distance < 3 or (distance == 3 and j < CHUNKS // 2):
+                go(ring_copy(sense, distance + 1, chunk))
+        if j == 0:
+            for sense, chunk in both:
                 tag_wait(sense, distance)
                 if distance < 3 or sense == 1:
                     go(tag_copy(sense, distance + 1))
-        expand_half(2 * distance - 1, right)
-        expand_half(2 * distance, left)
+        expand_chunk(2 * distance - 1, j)
+        expand_chunk(2 * distance, CHUNKS - 1 - j)
 
     def halo_forward(order):
         halo_wait(0, order, 1)
@@ -257,10 +245,12 @@
         go(halo_copy(3, order, 1, 1 + s, sibling))
         go(halo_copy(4, order, 5, 5 + s, sibling))
 
-    forward(1, True)
+    forward(1, 0)
     halo_forward(0)
-    forward(1, False)
+    forward(1, 1)
+    forward(1, 2)
     halo_forward(1)
+    forward(1, 3)
     expand_both(1)
     expand_both(5)
     for order in range(2):
@@ -292,13 +282,15 @@
     halo_wait(5, 0, 3 + 3 * s)
     expand_slot(3 + 3 * s, 1 - q)
     product_rows(near)
-    forward(2, True)
+    forward(2, 0)
     product_rows(near + 4)
+    forward(2, 1)
     halo_wait(5, 1, 3 + 3 * s)
     expand_slot(3 + 3 * s, q)
     product_rows(HALF * q)
-    forward(2, False)
+    forward(2, 2)
     product_rows(HALF * q + 4)
+    forward(2, 3)
 
     def group_of(t):
         return group(ORDER[t])
@@ -307,11 +299,11 @@
 
     def last_product():
         acc = jnp.zeros((WIDE, WIDE), F32)
-        for sub in range(2):
-            for sense, half in ((1, 0), (-1, 1)):
-                last_wait(sense, sub)
-                expand_half(LAST, half, sub * SUB, (sub + 1) * SUB)
-                rows = pl.ds((half * HALF + sub * SUB) * B, SUB * B)
+        for j in range(CHUNKS // 2):
+            for sense, chunk in ((1, j), (-1, CHUNKS - 1 - j)):
+                ring_wait(sense, 4, chunk)
+                expand_chunk(LAST, chunk)
+                rows = pl.ds(chunk * CHUNK * B, CHUNK * B)
                 acc += jnp.dot(turned[:, rows], wide[LAST, rows], preferred_element_type=F32)
         return acc
 
@@ -356,17 +348,19 @@
 
     window(0)
     early = len(sent)
-    forward(3, True)
+    forward(3, 0)
     window(1)
     finish(0)
     window(2)
+    forward(3, 1)
     finish(1)
     window(3)
     finish(2)
     window(4)
     finish(3)
     finish(4)
-    forward(3, False)
+    forward(3, 2)
+    forward(3, 3)
     window(5)
     window(6)
     finish(5)
@@ -406,7 +400,7 @@
             pltpu.VMEM((ROWS, K * B, B), BF16),
             pltpu.VMEM((SLOTS, 2, HALF * B + ROWS, B), BF16),
             pltpu.VMEM((SLOTS * ROWS, B, WIDE), BF16),
-            pltpu.VMEM((GROUPS, 2, HALF * B, B), BF16),
+            pltpu.VMEM((GROUPS, CHUNKS, CHUNK * B, B), BF16),
             pltpu.VMEM((GROUPS, ROWS, B), BF16),
             pltpu.VMEM((GROUPS, ROWS * B, WIDE), BF16),
             pltpu.VMEM((WIDE, ROWS * B), BF16),
@@ -423,16 +417,14 @@
             dma((4,)),
             dma((6, 2)),
             dma((6, 2)),
-            dma((2, 4, 2)),
-            dma((2, 4, 2)),
+            dma((2, 4, CHUNKS)),
+            dma((2, 4, CHUNKS)),
             dma((2, 4)),
             dma((2, 4)),
             dma((GROUPS,)),
             dma((GROUPS,)),
             dma((GROUPS, 2)),
             dma((CHIPS,)),
-            dma((2, 2)),
-            dma((2, 2)),
         ],
         compiler_params=pltpu.CompilerParams(
             collective_id=0, has_side_effects=True, vmem_limit_bytes=60 * 2**20

time: 62 us -> 61.3 us (0.989)
  Pallas kernels: 61.3 us -> 60.5 us
    pallas_call x1, Pallas kernels: 61.3 us -> 60.5 us  [body(): pl.pallas_call(kernel, out_shape=pltpu.VMEM((OUT, WIDE), F32), in_specs=[...]
where the time goes in v5:
time: 61.3 us; the launch traced here: 61.2 us
  Pallas kernels  60.5 us (99%)
  local copies, waits for them, and re-layouts  0.63 us (1%)
    pallas_call x1, Pallas kernels, body(): pl.pallas_call(kernel, out_shape=pltpu.VMEM((OUT, WIDE), F32), in_specs=[...  60.5 us

profile of v5, /device:TPU:5, one launch (start us, length us, event | category | flops | bytes accessed | tf_op | source)
XLA Modules:
  0.0 61.2 jit_solution(17515187990325530760)
XLA Ops:
  0.0 60.5 %shard_map.46 = f32[64,256]{1,0:T(8,128)S(1)} custom-call(s32[16,20]{1,0:T(8,128)} %fcol_hbm.1, s32[1,16]{1,0:T(1,128)} %bitcast.5, bf16[16,2560,128]{2,1,0:T(8,128)(2,1)} %bitcast.3, bf16[2048,128]{1,0:T(8,128)(2,1)} %bitcast.4), custom_call_target="tpu_custom_call" | custom-call | tf_op jit(solution)/shard_map/pallas_call | solution.py:394
  60.6 0.6 %copy.6 = f32[64,256]{1,0:T(8,128)} copy(f32[64,256]{1,0:T(8,128)S(1)} %shard_map.46) | data formatting | bytes 131072

commit v6 on v5

--- a/solution.py
+++ b/solution.py
@@ -75,6 +75,12 @@
 
     sibling = (r - s, z)
 
+    barrier = pltpu.get_barrier_semaphore()
+    peers = [(r, group(1)), (r, group(-1)), sibling, (2 * chip(s) + 1 - q, z)]
+    peers += [(2 * chip(j) + q, z) for j in range(1, CHIPS)]
+    for peer in peers:
+        pl.semaphore_signal(barrier, inc=1, device_id=peer, device_id_type=MESH)
+
     load_z = []
     for half in range(2):
         load_z.append(
@@ -89,17 +95,6 @@
     load_zcol.start()
     load_fcol = pltpu.make_async_copy(fcol_hbm, fcol, small_sem.at[1])
     load_fcol.start()
-    load_f = []
-    for g in range(4):
-        rows = pl.ds(4 * g, 4)
-        load_f.append(pltpu.make_async_copy(f_hbm.at[rows], fv.at[rows], f_sem.at[g]))
-        load_f[-1].start()
-
-    barrier = pltpu.get_barrier_semaphore()
-    peers = [(r, group(1)), (r, group(-1)), sibling, (2 * chip(s) + 1 - q, z)]
-    peers += [(2 * chip(j) + q, z) for j in range(1, CHIPS)]
-    for peer in peers:
-        pl.semaphore_signal(barrier, inc=1, device_id=peer, device_id_type=MESH)
 
     def remote(src, dst, send, recv, device):
         return pltpu.make_async_remote_copy(
@@ -191,6 +186,12 @@
     for j in range(1, CHUNKS):
         go(ring_copy(1, 1, j))
         go(ring_copy(-1, 1, CHUNKS - 1 - j))
+
+    load_f = []
+    for g in range(4):
+        rows = pl.ds(4 * g, 4)
+        load_f.append(pltpu.make_async_copy(f_hbm.at[rows], fv.at[rows], f_sem.at[g]))
+        load_f[-1].start()
 
     def expand_slot(slot, half):
         masks[...] = halo[slot, half, pl.ds(HALF * B, ROWS)].astype(F32)
@@ -346,13 +347,13 @@
             def _():
                 copy.start()
 
-    window(0)
     early = len(sent)
     forward(3, 0)
+    window(0)
     window(1)
+    forward(3, 1)
     finish(0)
     window(2)
-    forward(3, 1)
     finish(1)
     window(3)
     finish(2)

time: 61.3 us -> 61.2 us (level)
  no operation moved by 1% of the time
where the time goes in v6:
time: 61.2 us; the launch traced here: 61.1 us
  Pallas kernels  60.5 us (99%)
  local copies, waits for them, and re-layouts  0.63 us (1%)
    pallas_call x1, Pallas kernels, body(): pl.pallas_call(kernel, out_shape=pltpu.VMEM((OUT, WIDE), F32), in_specs=[...  60.5 us

profile of v6, /device:TPU:5, one launch (start us, length us, event | category | flops | bytes accessed | tf_op | source)
XLA Modules:
  0.0 61.1 jit_solution(7635365659243412112)
XLA Ops:
  0.0 60.5 %shard_map.46 = f32[64,256]{1,0:T(8,128)S(1)} custom-call(s32[16,20]{1,0:T(8,128)} %fcol_hbm.1, s32[1,16]{1,0:T(1,128)} %bitcast.5, bf16[16,2560,128]{2,1,0:T(8,128)(2,1)} %bitcast.3, bf16[2048,128]{1,0:T(8,128)(2,1)} %bitcast.4), custom_call_target="tpu_custom_call" | custom-call | tf_op jit(solution)/shard_map/pallas_call | solution.py:395
  60.5 0.6 %copy.6 = f32[64,256]{1,0:T(8,128)} copy(f32[64,256]{1,0:T(8,128)S(1)} %shard_map.46) | data formatting | bytes 131072

commit v7 on v6

--- a/solution.py
+++ b/solution.py
@@ -147,8 +147,18 @@
         ).wait_recv()
 
     pl.semaphore_wait(barrier, len(peers))
-    go(ring_copy(1, 1, 0))
-    go(ring_copy(-1, 1, CHUNKS - 1))
+    def own_chunk(j):
+        return [ring_copy(1, 1, j), ring_copy(-1, 1, CHUNKS - 1 - j)]
+
+    def start(copies):
+        for copy in copies:
+            copy.start()
+
+    def settle(copies):
+        for copy in copies:
+            copy.wait_send()
+
+    start(own_chunk(0))
 
     load_zcol.wait()
     load_fcol.wait()
@@ -178,14 +188,16 @@
     def halo_wait(step, order, slot):
         halo_copy(step, order, slot, slot, sibling, q if step < 2 else 1 - q).wait_recv()
 
-    for order in range(2):
-        go(halo_copy(0, order, OWN, 1, (2 * chip(1) + q, z)))
-        go(halo_copy(1, order, OWN, 5, (2 * chip(-1) + q, z)))
+    def own_half(order):
+        return [
+            halo_copy(0, order, OWN, 1, (2 * chip(1) + q, z)),
+            halo_copy(1, order, OWN, 5, (2 * chip(-1) + q, z)),
+        ]
+
+    start(own_half(0))
     for order in range(2):
         go(halo_copy(2, order, OWN, 3 + s, sibling))
-    for j in range(1, CHUNKS):
-        go(ring_copy(1, 1, j))
-        go(ring_copy(-1, 1, CHUNKS - 1 - j))
+    start(own_chunk(1))
 
     load_f = []
     for g in range(4):
@@ -209,9 +221,15 @@
         expand_slot(slot, 1)
 
     expand_both(OWN)
+    settle(own_chunk(0))
+    start(own_chunk(2))
     halo_wait(2, 0, 3 - s)
     halo_wait(2, 1, 3 - s)
     expand_both(3 - s)
+    settle(own_chunk(1))
+    start(own_chunk(3))
+    settle(own_half(0))
+    start(own_half(1))
 
     def expand_chunk(t, chunk):
         n = group(ORDER[t])
@@ -367,6 +385,7 @@
     finish(5)
     finish(6)
     drain(early)
+    settle(own_chunk(2) + own_chunk(3) + own_half(1))
     tag_wait(1, 4)
     window(7)
     finish(7)

time: 61.2 us -> 61.2 us (level)
  no operation moved by 1% of the time
where the time goes in v7:
time: 61.2 us; the launch traced here: 61.1 us
  Pallas kernels  60.5 us (99%)
  local copies, waits for them, and re-layouts  0.63 us (1%)
    pallas_call x1, Pallas kernels, body(): pl.pallas_call(kernel, out_shape=pltpu.VMEM((OUT, WIDE), F32), in_specs=[...  60.5 us

profile of v7, /device:TPU:5, one launch (start us, length us, event | category | flops | bytes accessed | tf_op | source)
XLA Modules:
  0.0 61.1 jit_solution(6843435976987883497)
XLA Ops:
  0.0 60.5 %shard_map.46 = f32[64,256]{1,0:T(8,128)S(1)} custom-call(s32[16,20]{1,0:T(8,128)} %fcol_hbm.1, s32[1,16]{1,0:T(1,128)} %bitcast.5, bf16[16,2560,128]{2,1,0:T(8,128)(2,1)} %bitcast.3, bf16[2048,128]{1,0:T(8,128)(2,1)} %bitcast.4), custom_call_target="tpu_custom_call" | custom-call | tf_op jit(solution)/shard_map/pallas_call | solution.py:414
  60.5 0.6 %copy.6 = f32[64,256]{1,0:T(8,128)} copy(f32[64,256]{1,0:T(8,128)S(1)} %shard_map.46) | data formatting | bytes 131072

commit v8 on v5

--- a/solution.py
+++ b/solution.py
@@ -303,14 +303,17 @@
             for sense, chunk in ((1, j), (-1, CHUNKS - 1 - j)):
                 ring_wait(sense, 4, chunk)
                 expand_chunk(LAST, chunk)
-                rows = pl.ds(chunk * CHUNK * B, CHUNK * B)
-                acc += jnp.dot(turned[:, rows], wide[LAST, rows], preferred_element_type=F32)
+                acc += part_product(LAST, chunk, 1)
         return acc
 
-    def window(t):
+    def part_product(t, first, count):
+        rows = pl.ds(first * CHUNK * B, count * CHUNK * B)
+        return jnp.dot(turned[:, rows], wide[t, rows], preferred_element_type=F32)
+
+    def window(t, product=None):
         if t == LAST:
             product = last_product()
-        else:
+        elif product is None:
             right = wide[t]
             if t == 0:
                 right = zexp[OWN * ROWS:(OWN + 1) * ROWS].reshape(ROWS * B, WIDE)
@@ -360,9 +363,11 @@
     finish(3)
     finish(4)
     forward(3, 2)
+    head5 = part_product(5, 0, CHUNKS - 1)
+    head6 = part_product(6, 1, CHUNKS - 1)
     forward(3, 3)
-    window(5)
-    window(6)
+    window(5, head5 + part_product(5, CHUNKS - 1, 1))
+    window(6, head6 + part_product(6, 0, 1))
     finish(5)
     finish(6)
     drain(early)

time: 61.3 us -> 61.3 us (level)
  no operation moved by 1% of the time
where the time goes in v8:
time: 61.3 us; the launch traced here: 61.2 us
  Pallas kernels  60.5 us (99%)
  local copies, waits for them, and re-layouts  0.63 us (1%)
    pallas_call x1, Pallas kernels, body(): pl.pallas_call(kernel, out_shape=pltpu.VMEM((OUT, WIDE), F32), in_specs=[...  60.5 us

profile of v8, /device:TPU:5, one launch (start us, length us, event | category | flops | bytes accessed | tf_op | source)
XLA Modules:
  0.0 61.2 jit_solution(12381734291659775338)
XLA Ops:
  0.0 60.5 %shard_map.46 = f32[64,256]{1,0:T(8,128)S(1)} custom-call(s32[16,20]{1,0:T(8,128)} %fcol_hbm.1, s32[1,16]{1,0:T(1,128)} %bitcast.5, bf16[16,2560,128]{2,1,0:T(8,128)(2,1)} %bitcast.3, bf16[2048,128]{1,0:T(8,128)(2,1)} %bitcast.4), custom_call_target="tpu_custom_call" | custom-call | tf_op jit(solution)/shard_map/pallas_call | solution.py:399
  60.6 0.6 %copy.6 = f32[64,256]{1,0:T(8,128)} copy(f32[64,256]{1,0:T(8,128)S(1)} %shard_map.46) | data formatting | bytes 131072

commit v9 on v5

--- a/solution.py
+++ b/solution.py
@@ -368,7 +368,17 @@
     drain(early)
     tag_wait(1, 4)
     window(7)
+    drain(len(sent) - 1)
     finish(7)
+
+    drain(len(sent))
+    for t in range(GROUPS):
+        for h in range(2):
+            d, copy = sum_copy(t, h)
+
+            @pl.when(d != m)
+            def _():
+                copy.wait_send()
 
     acc = total[...]
     for j in range(1, CHIPS):
@@ -378,15 +388,6 @@
         ).wait_recv()
         acc += arrived[source].astype(F32)
     out[...] = acc
-
-    drain(len(sent))
-    for t in range(GROUPS):
-        for h in range(2):
-            d, copy = sum_copy(t, h)
-
-            @pl.when(d != m)
-            def _():
-                copy.wait_send()
 
 
 def body(fblocks, fcol, zblocks, zcol):

time: 61.3 us -> 61.2 us (level)
  no operation moved by 1% of the time
where the time goes in v9:
time: 61.2 us
  Pallas kernels  60.5 us (99%)
  local copies, waits for them, and re-layouts  0.63 us (1%)
    pallas_call x1, Pallas kernels, body(): pl.pallas_call(kernel, out_shape=pltpu.VMEM((OUT, WIDE), F32), in_specs=[...  60.5 us

profile of v9, /device:TPU:5, one launch (start us, length us, event | category | flops | bytes accessed | tf_op | source)
XLA Modules:
  0.0 61.2 jit_solution(13329096146598980018)
XLA Ops:
  0.0 60.5 %shard_map.46 = f32[64,256]{1,0:T(8,128)S(1)} custom-call(s32[16,20]{1,0:T(8,128)} %fcol_hbm.1, s32[1,16]{1,0:T(1,128)} %bitcast.5, bf16[16,2560,128]{2,1,0:T(8,128)(2,1)} %bitcast.3, bf16[2048,128]{1,0:T(8,128)(2,1)} %bitcast.4), custom_call_target="tpu_custom_call" | custom-call | tf_op jit(solution)/shard_map/pallas_call | solution.py:395
  60.5 0.6 %copy.6 = f32[64,256]{1,0:T(8,128)} copy(f32[64,256]{1,0:T(8,128)S(1)} %shard_map.46) | data formatting | bytes 131072

commit v10 on v5

--- a/solution.py
+++ b/solution.py
@@ -60,6 +60,8 @@
     pair_recv,
     sum_send,
     sum_recv,
+    last_send,
+    last_recv,
 ):
     r = lax.axis_index("rows")
     z = lax.axis_index("cols")
@@ -297,24 +299,36 @@
 
     pair_copies = []
 
-    def last_product():
-        acc = jnp.zeros((WIDE, WIDE), F32)
+    def last_copy(h):
+        return remote(
+            part.at[LAST, 1 - q, h], other.at[LAST, h], last_send.at[h], last_recv.at[h], sibling
+        )
+
+    def last_window():
+        accs = [jnp.zeros((WIDE, B), F32)] * 2
         for j in range(CHUNKS // 2):
-            for sense, chunk in ((1, j), (-1, CHUNKS - 1 - j)):
+            both = ((1, j), (-1, CHUNKS - 1 - j))
+            for sense, chunk in both:
                 ring_wait(sense, 4, chunk)
                 expand_chunk(LAST, chunk)
-                rows = pl.ds(chunk * CHUNK * B, CHUNK * B)
-                acc += jnp.dot(turned[:, rows], wide[LAST, rows], preferred_element_type=F32)
-        return acc
+            for h in range(2):
+                for _, chunk in both:
+                    rows = pl.ds(chunk * CHUNK * B, CHUNK * B)
+                    accs[h] += jnp.dot(
+                        turned[:, rows], wide[LAST, rows, h * B:(h + 1) * B],
+                        preferred_element_type=F32,
+                    )
+                if j == CHUNKS // 2 - 1:
+                    product = jnp.transpose(accs[h])
+                    for core in range(2):
+                        part[LAST, core, h] = product[core * OUT:(core + 1) * OUT]
+                    go(last_copy(h))
 
     def window(t):
-        if t == LAST:
-            product = last_product()
-        else:
-            right = wide[t]
-            if t == 0:
-                right = zexp[OWN * ROWS:(OWN + 1) * ROWS].reshape(ROWS * B, WIDE)
-            product = jnp.dot(turned[...], right, preferred_element_type=F32)
+        right = wide[t]
+        if t == 0:
+            right = zexp[OWN * ROWS:(OWN + 1) * ROWS].reshape(ROWS * B, WIDE)
+        product = jnp.dot(turned[...], right, preferred_element_type=F32)
         product = jnp.transpose(product)
         for b in range(4):
             part[t, b % 2, b // 2] = product[b * OUT:(b + 1) * OUT]
@@ -332,8 +346,11 @@
         )
 
     def finish(t):
-        pair_copies[t].wait_recv()
+        if t != LAST:
+            pair_copies[t].wait_recv()
         for h in range(2):
+            if t == LAST:
+                last_copy(h).wait_recv()
             both = part[t, q, h] + other[t, h]
             chip_sum[t, h] = both.astype(BF16)
             d, copy = sum_copy(t, h)
@@ -367,7 +384,7 @@
     finish(6)
     drain(early)
     tag_wait(1, 4)
-    window(7)
+    last_window()
     finish(7)
 
     acc = total[...]
@@ -425,6 +442,8 @@
             dma((GROUPS,)),
             dma((GROUPS, 2)),
             dma((CHIPS,)),
+            dma((2,)),
+            dma((2,)),
         ],
         compiler_params=pltpu.CompilerParams(
             collective_id=0, has_side_effects=True, vmem_limit_bytes=60 * 2**20

time: 61.3 us -> 61.6 us (level)
  no operation moved by 1% of the time
where the time goes in v10:
time: 61.6 us; the launch traced here: 61.5 us
  Pallas kernels  60.9 us (99%)
  local copies, waits for them, and re-layouts  0.63 us (1%)
    pallas_call x1, Pallas kernels, body(): pl.pallas_call(kernel, out_shape=pltpu.VMEM((OUT, WIDE), F32), in_specs=[...  60.9 us

profile of v10, /device:TPU:5, one launch (start us, length us, event | category | flops | bytes accessed | tf_op | source)
XLA Modules:
  0.0 61.5 jit_solution(15431027590024319361)
XLA Ops:
  0.0 60.9 %shard_map.46 = f32[64,256]{1,0:T(8,128)S(1)} custom-call(s32[16,20]{1,0:T(8,128)} %fcol_hbm.1, s32[1,16]{1,0:T(1,128)} %bitcast.5, bf16[16,2560,128]{2,1,0:T(8,128)(2,1)} %bitcast.3, bf16[2048,128]{1,0:T(8,128)(2,1)} %bitcast.4), custom_call_target="tpu_custom_call" | custom-call | tf_op jit(solution)/shard_map/pallas_call | solution.py:411
  60.9 0.6 %copy.6 = f32[64,256]{1,0:T(8,128)} copy(f32[64,256]{1,0:T(8,128)S(1)} %shard_map.46) | data formatting | bytes 131072
